TPU v7x, 32 devices: a whole 2x2x4 slice. The times are simulated.
32 devices in a mesh: dp: 4 (over y, x), expert: 8 (over z, core).
Axes of the slice: x: 2, y: 2, z: 4, core: 2. Of those that a mesh axis runs over, the one named last changes fastest.
Arguments:
- tokens: bfloat16 [4096, 1536], P(('dp', 'expert')), may hold values from -6 to 6
- gate_prob: float32 [4096], P(('dp', 'expert')), may hold values from 0.2 to 1
- expert_index: int32 [4096], P(('dp', 'expert')), may hold values from 0 to 15, as said below
- slot_index: int32 [4096], P(('dp', 'expert')), may hold values from 0 to 127, as said below
- dropped: int32 [4096], P(('dp', 'expert')), may hold values from 0 to 1
- cotangent: bfloat16 [4096, 1536], P(('dp', 'expert')), may hold values from -6 to 6
- expert_in: bfloat16 [16, 1536, 6144], P('expert', None, 'dp'), may hold values from -0.15625 to 0.15625
- expert_out: bfloat16 [16, 6144, 1536], P('expert', 'dp'), may hold values from -0.078125 to 0.078125
- residual_in: bfloat16 [1536, 3072], P(None, 'dp'), may hold values from -0.15625 to 0.15625
- residual_out: bfloat16 [3072, 1536], P('dp'), may hold values from -0.109375 to 0.109375
Outputs:
- output: bfloat16 [4096, 1536], P(('dp', 'expert'))
- grad_tokens: bfloat16 [4096, 1536], P(('dp', 'expert'))
- grad_gate: float32 [4096], P(('dp', 'expert'))
- grad_expert_in: bfloat16 [16, 1536, 6144], P('expert', None, 'dp')
- grad_expert_out: bfloat16 [16, 6144, 1536], P('expert', 'dp')
- grad_residual_in: bfloat16 [1536, 3072], P(None, 'dp')
- grad_residual_out: bfloat16 [3072, 1536], P('dp')
Inputs may be any that keep to these rules, and one draw needn't show every extreme that they name: `expert_index`: on every device, at least 12 tokens choose one expert, the same expert on all devices, and the tokens in its first 10 slots are not dropped. `slot_index`: on each device the tokens of one expert hold the slots 0 to n - 1 once each, n being their count; dropped tokens take the highest slots of their expert; on some device all tokens choose one expert.
All inputs are finite; a program needn't handle non-finite values.
Results may differ from a plain program's by a relative error of at most 0.018.
Values may be sent and summed in bfloat16 or wider, within the bound.
A program may use at most 192 MiB of HBM per device.

v0:
```python
import jax
import jax.numpy as jnp
from jax import lax
from jax.sharding import PartitionSpec as P


def gelu_tanh(values):
    return jax.nn.gelu(values, approximate=True)


def place_rows(values, position, slot_count):
    buffer = jnp.zeros((slot_count + 1, values.shape[1]), values.dtype)
    return buffer.at[position].set(values)[:slot_count]


def fetch_rows(buffer, position):
    padded = jnp.concatenate([buffer, jnp.zeros((1, buffer.shape[1]), buffer.dtype)], axis=0)
    return padded[position]


def on_device(
    tokens,
    gate_prob,
    expert_index,
    slot_index,
    dropped,
    cotangent,
    expert_in,
    expert_out,
    residual_in,
    residual_out,
):
    groups = lax.axis_size("dp")
    host_count = lax.axis_size("expert")
    local_count = expert_in.shape[0]
    experts_all = local_count * host_count
    row_count, model_width = tokens.shape
    capacity = max(2, 5 * row_count // (4 * experts_all))
    kept = (dropped == 0) & (slot_index < capacity)
    kept_float = kept.astype(jnp.float32)
    gate_kept = gate_prob * kept_float
    own_slots = experts_all * capacity
    own_index = jnp.where(kept, expert_index * capacity + slot_index, -1)
    own_position = jnp.where(kept, own_index, own_slots)

    def to_column(row_values, row_scale):
        values = (row_values.astype(jnp.float32) * row_scale[:, None]).astype(jnp.bfloat16)
        own_buffer = place_rows(values, own_position, own_slots).reshape(
            host_count, local_count, capacity, model_width
        )
        arrived = lax.all_to_all(own_buffer, "expert", split_axis=0, concat_axis=0, tiled=True)
        col_rows, column = (
            lax.all_gather(row_values, "dp", axis=0, tiled=True),
            lax.all_gather(arrived[None], "dp", axis=0, tiled=True),
        )
        return (col_rows, column)

    def from_column(dense_part, expert_part):
        dense_sum, expert_sum = (
            lax.psum_scatter(
                dense_part.astype(jnp.bfloat16), "dp", scatter_dimension=0, tiled=True
            ).astype(jnp.float32),
            lax.psum_scatter(
                expert_part.astype(jnp.bfloat16), "dp", scatter_dimension=0, tiled=True
            ).astype(jnp.float32),
        )
        own_result = lax.all_to_all(
            expert_sum[0].astype(jnp.bfloat16), "expert", split_axis=0, concat_axis=0, tiled=True
        )
        return (dense_sum[0], own_result.reshape(own_slots, model_width))

    unit_scale = jnp.ones_like(gate_prob)
    col_tokens, column = to_column(tokens, unit_scale)
    pre_expert = jnp.einsum(
        "abjcd,jdf->abjcf", column, expert_in, preferred_element_type=jnp.float32
    )
    hidden_f, expert_back = jax.vjp(gelu_tanh, pre_expert)
    hidden = hidden_f.astype(jnp.bfloat16)
    expert_part = jnp.einsum(
        "abjcf,jfd->abjcd", hidden, expert_out, preferred_element_type=jnp.float32
    )
    pre_dense = jnp.dot(col_tokens, residual_in, preferred_element_type=jnp.float32)
    dense_f, dense_back = jax.vjp(gelu_tanh, pre_dense)
    dense_hidden = dense_f.astype(jnp.bfloat16)
    dense_part = jnp.dot(dense_hidden, residual_out, preferred_element_type=jnp.float32).reshape(
        groups, row_count, model_width
    )
    dense_sum, expert_rows = from_column(dense_part, expert_part)
    expert_token = fetch_rows(expert_rows, own_position).astype(jnp.float32)
    output = (dense_sum + gate_kept[:, None] * expert_token).astype(jnp.bfloat16)
    grad_gate = kept_float * jnp.sum(cotangent.astype(jnp.float32) * expert_token, axis=1)
    col_cotangent, grad_column = to_column(cotangent, gate_kept)
    grad_hidden = jnp.einsum(
        "abjcd,jfd->abjcf", grad_column, expert_out, preferred_element_type=jnp.float32
    )
    grad_pre = expert_back(grad_hidden)[0].astype(jnp.bfloat16)
    grad_expert_out = jnp.einsum(
        "abjcf,abjcd->jfd", hidden, grad_column, preferred_element_type=jnp.float32
    ).astype(jnp.bfloat16)
    grad_expert_in = jnp.einsum(
        "abjcd,abjcf->jdf", column, grad_pre, preferred_element_type=jnp.float32
    ).astype(jnp.bfloat16)
    expert_dx = jnp.einsum(
        "abjcf,jdf->abjcd", grad_pre, expert_in, preferred_element_type=jnp.float32
    )
    dense_grad_hidden = jnp.einsum(
        "td,fd->tf", col_cotangent, residual_out, preferred_element_type=jnp.float32
    )
    dense_grad_pre = dense_back(dense_grad_hidden)[0].astype(jnp.bfloat16)
    out_partial = jnp.einsum(
        "tf,td->fd", dense_hidden, col_cotangent, preferred_element_type=jnp.float32
    )
    in_partial = jnp.einsum(
        "td,tf->df", col_tokens, dense_grad_pre, preferred_element_type=jnp.float32
    )
    in_total, out_total = (
        lax.psum(in_partial.astype(jnp.bfloat16), "expert").astype(jnp.float32),
        lax.psum(out_partial.astype(jnp.bfloat16), "expert").astype(jnp.float32),
    )
    dense_dx = jnp.einsum(
        "tf,df->td", dense_grad_pre, residual_in, preferred_element_type=jnp.float32
    ).reshape(groups, row_count, model_width)
    dense_dx_sum, expert_dx_rows = from_column(dense_dx, expert_dx)
    grad_tokens = (
        dense_dx_sum + fetch_rows(expert_dx_rows, own_position).astype(jnp.float32)
    ).astype(jnp.bfloat16)
    return (
        output,
        grad_tokens,
        grad_gate,
        grad_expert_in,
        grad_expert_out,
        in_total.astype(jnp.bfloat16),
        out_total.astype(jnp.bfloat16),
    )


def solution(mesh):
    return jax.shard_map(
        on_device,
        mesh=mesh,
        in_specs=(
            P(("dp", "expert"), None),
            P(("dp", "expert")),
            P(("dp", "expert")),
            P(("dp", "expert")),
            P(("dp", "expert")),
            P(("dp", "expert"), None),
            P("expert", None, "dp"),
            P("expert", "dp", None),
            P(None, "dp"),
            P("dp", None),
        ),
        out_specs=(
            P(("dp", "expert"), None),
            P(("dp", "expert"), None),
            P(("dp", "expert")),
            P("expert", None, "dp"),
            P("expert", "dp", None),
            P(None, "dp"),
            P("dp", None),
        ),
        check_vma=False,
    )
```

profile of v0, /device:TPU:9, one launch (start us, length us, event | category | flops | bytes accessed | tf_op | source)
XLA Modules:
  0.0 439.4 jit_solution(6969750506821236974)
XLA Ops:
  12.5 17.3 %all_to_all.20 = bf16[8,2,10,1536]{3,1,2,0:T(2,128)(2,1)} all-to-all(bf16[8,2,10,1536]{3,1,2,0:T(2,128)(2,1)S(1)} %copy.38), channel_id=1, replica_groups=mesh['dp'=4,'expert'=8] {'expert'}, dimensions={0} | all-to-all | bytes 983040 | tf_op jit(solution)/shard_map/all_to_all | solution.py:51
  33.9 17.7 %all_to_all.21 = bf16[8,2,10,1536]{3,1,2,0:T(2,128)(2,1)} all-to-all(bf16[8,2,10,1536]{3,1,2,0:T(2,128)(2,1)S(1)} %copy.45), channel_id=1, replica_groups=mesh['dp'=4,'expert'=8] {'expert'}, dimensions={0} | all-to-all | bytes 983040 | tf_op jit(solution)/shard_map/all_to_all | solution.py:51
  53.2 12.0 %all-gather.11.cloned.1.call-done = bf16[32,2,10,1536]{3,1,2,0:T(2,128)(2,1)} async-done(((bf16[8,2,10,1536]{3,1,2,0:T(2,128)(2,1)}), bf16[32,2,10,1536]{3,1,2,0:T(2,128)(2,1)}) %all-gather.11.cloned.1.call-update) | async-done | bytes 1966096 | tf_op jit(solution)/shard_map/all_gather | solution.py:54
  68.9 9.5 %fusion.18 = (bf16[4,8,2,10,1536]{4,1,3,2,0:T(8,128)(2,1)}, f32[2,4,8,10,1536]{4,2,3,0,1:T(8,128)}) fusion(bf16[2,1536,1536]{2,1,0:T(8,128)(2,1)} %param.16, bf16[4,8,2,10,1536]{4,3,1,0,2:T(8,128)(2,1)S(1)} %bitcast.96), kind=kOutput, calls=%fused_computation.29 | convolution fusion | flops 3028746240 | bytes 17301504 | tf_op jit(solution)/shard_map/abjcd,jdf->abjcf/dot_general | solution.py:74
  78.4 22.8 %all-gather.13.cloned.1.call-done = bf16[32,2,10,1536]{3,1,2,0:T(2,128)(2,1)} async-done(((bf16[8,2,10,1536]{3,1,2,0:T(2,128)(2,1)}), bf16[32,2,10,1536]{3,1,2,0:T(2,128)(2,1)}) %all-gather.13.cloned.1.call-update) | async-done | bytes 1966096 | tf_op jit(solution)/shard_map/all_gather | solution.py:54
  103.4 13.9 %fusion.14 = bf16[4,8,2,10,1536]{4,1,3,2,0:T(8,128)(2,1)} fusion(f32[2,4,8,10,1536]{4,2,3,0,1:T(8,128)} %get-tuple-element.40, bf16[2,1536,1536]{2,1,0:T(8,128)(2,1)} %param.17, bf16[4,8,2,10,1536]{4,3,1,0,2:T(8,128)(2,1)S(1)} %bitcast.98), kind=kOutput, calls=%fused_computation.22 | convolution fusion | flops 3039559680 | bytes 17301504 | tf_op jit(solution)/shard_map/abjcd,jfd->abjcf/dot_general | solution.py:93
  117.3 9.3 %fusion.27 = bf16[4,8,2,10,1536]{4,3,1,0,2:T(8,128)(2,1)S(1)} fusion(bf16[2,1536,1536]{2,1,0:T(8,128)(2,1)} %param.16, bf16[4,8,2,10,1536]{4,1,3,2,0:T(8,128)(2,1)} %fusion.14), kind=kOutput, calls=%fused_computation.34 | convolution fusion | flops 3020881920 | bytes 13369344 | tf_op jit(solution)/shard_map/abjcf,jdf->abjcd/dot_general | solution.py:103
  129.3 9.3 %fusion.30 = bf16[4,8,2,10,1536]{4,3,1,0,2:T(8,128)(2,1)S(1)} fusion(bf16[2,1536,1536]{2,1,0:T(8,128)(2,1)} %param.17, bf16[4,8,2,10,1536]{4,1,3,2,0:T(8,128)(2,1)} %get-tuple-element.39), kind=kOutput, calls=%fused_computation.35 | convolution fusion | flops 3020881920 | bytes 13369344 | tf_op jit(solution)/shard_map/abjcf,jfd->abjcd/dot_general | solution.py:79
  141.1 4.8 %fusion.59 = f32[512,768]{1,0:T(8,128)} fusion(bf16[512,1536]{1,0:T(8,128)(2,1)} %all-gather.9.cloned.1.call-done, bf16[768,1536]{1,0:T(8,128)(2,1)} %param.19), kind=kOutput, calls=%fused_computation.76 | convolution fusion | flops 1207959552 | bytes 5505024 | tf_op jit(solution)/shard_map/td,fd->tf/dot_general | solution.py:106
  145.8 21.0 %all-gather.7.cloned.1.call-done = bf16[512,1536]{1,0:T(8,128)(2,1)} async-done(((bf16[128,1536]{1,0:T(8,128)(2,1)}), bf16[512,1536]{1,0:T(8,128)(2,1)}) %all-gather.7.cloned.1.call-update) | async-done | bytes 1572880 | tf_op jit(solution)/shard_map/all_gather | solution.py:53
  166.8 4.1 fusion.45
  173.8 2.9 convolution_convert_fusion
  176.8 5.0 %convolution_convert_fusion.3 = bf16[512,1536]{1,0:T(8,128)(2,1)} fusion(bf16[768,1536]{1,0:T(8,128)(2,1)} %param.19, f32[512,768]{1,0:T(8,128)} %copy-done.16), kind=kOutput, calls=%fused_computation.42 | convolution fusion | flops 1212284928 | bytes 5505024 | tf_op jit(solution)/shard_map/dot_general | solution.py:85
  185.1 19.3 %reduce-scatter.19.cloned.1.call-done = bf16[1,8,2,10,1536]{4,1,3,2,0:T(8,128)(2,1)} async-done(((bf16[4,8,2,10,1536]{4,1,3,2,0:T(8,128)(2,1)}), bf16[1,8,2,10,1536]{4,1,3,2,0:T(8,128)(2,1)}) %reduce-scatter.19.cloned.1.call-update) | async-done | bytes 491536
  206.7 5.5 %all-to-all-start.3 = ((bf16[8,2,10,1536]{3,1,2,0:T(2,128)(2,1)}), bf16[8,2,10,1536]{3,1,2,0:T(2,128)(2,1)}, u32[]{:S(2)}, u32[]{:S(2)}) async-start(bf16[8,2,10,1536]{3,1,2,0:T(2,128)(2,1)} %copy.50), calls=%async_computation.3 | async-start | bytes 983040 | tf_op jit(solution)/shard_map/all_to_all | solution.py:67
  212.2 10.1 %bitcast_convert_fusion = bf16[2,1536,1536]{2,1,0:T(8,128)(2,1)} fusion(bf16[4,8,2,10,1536]{4,1,3,2,0:T(8,128)(2,1)} %get-tuple-element.39, bf16[4,8,2,10,1536]{4,3,1,0,2:T(8,128)(2,1)} %bitcast.99), kind=kOutput, calls=%fused_computation.4 | convolution fusion | flops 3024617472 | bytes 13369344 | tf_op jit(solution)/shard_map/abjcf,abjcd->jfd/dot_general | solution.py:97
  222.3 19.2 %reduce-scatter.15.cloned.1.call-done = bf16[1,8,2,10,1536]{4,1,3,2,0:T(8,128)(2,1)} async-done(((bf16[4,8,2,10,1536]{4,1,3,2,0:T(8,128)(2,1)}), bf16[1,8,2,10,1536]{4,1,3,2,0:T(8,128)(2,1)}) %reduce-scatter.15.cloned.1.call-update) | async-done | bytes 491536
  243.8 5.5 %all-to-all-start.1 = ((bf16[8,2,10,1536]{3,1,2,0:T(2,128)(2,1)}), bf16[8,2,10,1536]{3,1,2,0:T(2,128)(2,1)}, u32[]{:S(2)}, u32[]{:S(2)}) async-start(bf16[8,2,10,1536]{3,1,2,0:T(2,128)(2,1)} %copy.43), calls=%async_computation.1 | async-start | bytes 983040 | tf_op jit(solution)/shard_map/all_to_all | solution.py:67
  249.3 9.5 %bitcast_convert_fusion.1 = bf16[2,1536,1536]{2,1,0:T(8,128)(2,1)} fusion(bf16[4,8,2,10,1536]{4,1,3,2,0:T(8,128)(2,1)} %fusion.14, bf16[4,8,2,10,1536]{4,3,1,0,2:T(8,128)(2,1)S(1)} %bitcast.97), kind=kOutput, calls=%fused_computation.5 | convolution fusion | flops 3024617472 | bytes 13369344 | tf_op jit(solution)/shard_map/abjcd,abjcf->jdf/dot_general | solution.py:100
  258.8 100.8 %all-reduce.9.cloned.1.call-done = (bf16[1536,768]{0,1:T(8,128)(2,1)}, bf16[768,1536]{1,0:T(8,128)(2,1)}) async-done(((bf16[1536,768]{0,1:T(8,128)(2,1)}, bf16[768,1536]{1,0:T(8,128)(2,1)}), (bf16[1536,768]{0,1:T(8,128)(2,1)}, bf16[768,1536]{1,0:T(8,128)(2,1)})) %all-reduce.9.cloned.1.call-update) | async-done | bytes 4718608 | tf_op jit(solution)/shard_map/psum | solution.py:117
  359.6 4.3 copy.56
  368.9 24.8 %reduce-scatter.13.cloned.1.call-done = bf16[1,128,1536]{2,1,0:T(8,128)(2,1)} async-done(((bf16[4,128,1536]{2,1,0:T(8,128)(2,1)}), bf16[1,128,1536]{2,1,0:T(8,128)(2,1)}) %reduce-scatter.13.cloned.1.call-update) | async-done | bytes 393232
  396.2 31.4 %reduce-scatter.17.cloned.1.call-done = bf16[1,128,1536]{2,1,0:T(8,128)(2,1)} async-done(((bf16[4,128,1536]{2,1,0:T(8,128)(2,1)}), bf16[1,128,1536]{2,1,0:T(8,128)(2,1)}) %reduce-scatter.17.cloned.1.call-update) | async-done | bytes 393232
  429.5 3.4 copy.88
  (85 shorter events, 41.9 us)
Async XLA Ops:
  7.2 159.7 %copy-start = (bf16[1536,768]{1,0:T(8,128)(2,1)S(1)}, bf16[1536,768]{1,0:T(8,128)(2,1)}, u32[]{:S(2)}) copy-start(bf16[1536,768]{1,0:T(8,128)(2,1)} %param.18) | copy-start | bytes 7077892
  7.2 57.9 %all-gather.11.cloned.1.call-start = ((), (), s32[]{:S(2)}) async-start(), calls=%async_computation.10 | async-start | bytes 2457600 | tf_op jit(solution)/shard_map/all_gather | solution.py:54
  9.9 20.0 %copy-start.9 = (s32[128]{0:T(128)S(1)}, s32[128]{0:T(128)}, u32[]{:S(2)}) copy-start(s32[128]{0:T(128)} %param.13) | copy-start | bytes 1540
  9.9 20.0 %copy-start.11 = (s32[128]{0:T(128)S(1)}, s32[128]{0:T(128)}, u32[]{:S(2)}) copy-start(s32[128]{0:T(128)} %param.14) | copy-start | bytes 1540
  9.9 20.0 %copy-start.13 = (f32[128]{0:T(128)S(1)}, f32[128]{0:T(128)}, u32[]{:S(2)}) copy-start(f32[128]{0:T(128)} %param.11) | copy-start | bytes 1540
  9.9 20.0 %copy-start.2 = (bf16[128,1536]{1,0:T(8,128)(2,1)S(1)}, bf16[128,1536]{1,0:T(8,128)(2,1)}, u32[]{:S(2)}) copy-start(bf16[128,1536]{1,0:T(8,128)(2,1)} %param.15) | copy-start | bytes 1179652
  29.8 71.4 %all-gather.13.cloned.1.call-start = ((), (), s32[]{:S(2)}) async-start(), calls=%async_computation.11 | async-start | bytes 2457600 | tf_op jit(solution)/shard_map/all_gather | solution.py:54
  29.9 21.7 %copy-start.7 = (f32[128]{0:T(128)}, f32[128]{0:T(128)S(1)}, u32[]{:S(2)}) copy-start(f32[128]{0:T(128)S(1)} %broadcast_select_fusion.1) | copy-start | bytes 1540
  51.6 89.4 %all-gather.9.cloned.1.call-start = ((), (), s32[]{:S(2)}) async-start(), calls=%async_computation.9 | async-start | bytes 1966080 | tf_op jit(solution)/shard_map/all_gather | solution.py:53
  52.4 114.5 %all-gather.7.cloned.1.call-start = ((), (), s32[]{:S(2)}) async-start(), calls=%async_computation.8 | async-start | bytes 1966080 | tf_op jit(solution)/shard_map/all_gather | solution.py:53
  52.9 151.5 %reduce-scatter.19.cloned.1.call-start = ((), (), s32[]{:S(2)}) async-start(), calls=%async_computation.15 | async-start | bytes 2457600
  103.4 13.9 %copy-start.6 = (bf16[32,2,10,1536]{3,2,0,1:T(8,128)(2,1)}, bf16[32,2,10,1536]{3,2,0,1:T(8,128)(2,1)S(1)}, u32[]{:S(2)}) copy-start(bf16[32,2,10,1536]{3,2,0,1:T(8,128)(2,1)S(1)} %copy.46) | copy-start | bytes 5898244
  129.0 112.5 %reduce-scatter.15.cloned.1.call-start = ((), (), s32[]{:S(2)}) async-start(), calls=%async_computation.13 | async-start | bytes 2457600
  141.0 218.6 %all-reduce.9.cloned.1.call-start = ((), (), s32[]{:S(2)}) async-start(), calls=%async_computation.16 | async-start | bytes 9437184 | tf_op jit(solution)/shard_map/psum | solution.py:117
  166.8 4.2 copy-start.15
  176.8 216.9 %reduce-scatter.13.cloned.1.call-start = ((), (), s32[]{:S(2)}) async-start(), calls=%async_computation.12 | async-start | bytes 1966080
  181.9 245.8 %reduce-scatter.17.cloned.1.call-start = ((), (), s32[]{:S(2)}) async-start(), calls=%async_computation.14 | async-start | bytes 1966080
  206.7 37.1 %all-to-all-start.3 = ((bf16[8,2,10,1536]{3,1,2,0:T(2,128)(2,1)}), bf16[8,2,10,1536]{3,1,2,0:T(2,128)(2,1)}, u32[]{:S(2)}, u32[]{:S(2)}) async-start(bf16[8,2,10,1536]{3,1,2,0:T(2,128)(2,1)} %copy.50), calls=%async_computation.3 | async-start | bytes 983040 | tf_op jit(solution)/shard_map/all_to_all | solution.py:67
  212.2 37.1 %copy-start.5 = (bf16[32,2,10,1536]{3,2,0,1:T(8,128)(2,1)S(1)}, bf16[32,2,10,1536]{3,2,0,1:T(8,128)(2,1)}, u32[]{:S(2)}) copy-start(bf16[32,2,10,1536]{3,2,0,1:T(8,128)(2,1)} %copy-done.4) | copy-start | bytes 5898244
  243.8 121.5 %all-to-all-start.1 = ((bf16[8,2,10,1536]{3,1,2,0:T(2,128)(2,1)}), bf16[8,2,10,1536]{3,1,2,0:T(2,128)(2,1)}, u32[]{:S(2)}, u32[]{:S(2)}) async-start(bf16[8,2,10,1536]{3,1,2,0:T(2,128)(2,1)} %copy.43), calls=%async_computation.1 | async-start | bytes 983040 | tf_op jit(solution)/shard_map/all_to_all | solution.py:67
  367.7 26.0 %copy-start.3 = (bf16[128,1536]{1,0:T(8,128)(2,1)S(1)}, bf16[128,1536]{1,0:T(8,128)(2,1)}, u32[]{:S(2)}) copy-start(bf16[128,1536]{1,0:T(8,128)(2,1)} %param.15) | copy-start | bytes 1179652
  367.7 26.0 %copy-start.8 = (f32[128]{0:T(128)S(1)}, f32[128]{0:T(128)}, u32[]{:S(2)}) copy-start(f32[128]{0:T(128)} %copy-done.7) | copy-start | bytes 1540
  367.7 28.0 %copy-start.10 = (s32[128]{0:T(128)S(1)}, s32[128]{0:T(128)}, u32[]{:S(2)}) copy-start(s32[128]{0:T(128)} %param.13) | copy-start | bytes 1540
  367.7 28.0 %copy-start.12 = (s32[128]{0:T(128)S(1)}, s32[128]{0:T(128)}, u32[]{:S(2)}) copy-start(s32[128]{0:T(128)} %param.14) | copy-start | bytes 1540
  (4 other events, 10.7 us)
Sparse Core Ops, SparseCore 0:
  29.9 35.1 all-gather.10
  67.0 34.2 all-gather.12
  103.1 30.9 all-gather.8
  135.8 30.9 all-gather.6
  170.3 34.0 reduce-scatter.18
  207.4 34.0 reduce-scatter.14
  244.5 115.1 all-reduce.8
  362.6 31.0 reduce-scatter.12
  396.7 30.9 reduce-scatter.16
where the time goes:
time: 442 us; the launch traced here: 439 us
  waiting for transfers between devices  253 us (57%)
  matrix products  83.8 us (19%)
  blocking collectives  35.1 us (8%)
  local copies, waits for them, and re-layouts  34.8 us (8%)
  between operations  14.2 us (3%)
  starting transfers between devices  11.7 us (3%)
  other arithmetic  7.2 us (2%)
    psum x1, waiting for transfers between devices, on_device(): lax.psum(in_partial.astype(jnp.bfloat16), 'expert').astype(jnp.float32)  101 us
    unnamed x13, waiting for transfers between devices  96.1 us
    all_to_all x2, blocking collectives, to_column(): lax.all_to_all(own_buffer, 'expert', split_axis=0, concat_axis=0, tiled=T...  35.1 us
    all_gather x2, waiting for transfers between devices, to_column(): lax.all_gather(arrived[None], 'dp', axis=0, tiled=True)  34.7 us
    all_gather x2, waiting for transfers between devices, to_column(): lax.all_gather(row_values, 'dp', axis=0, tiled=True)  21 us
    dot_general x1, matrix products, on_device(): jnp.einsum('abjcd,jfd->abjcf', grad_column, expert_out, preferred_element...  13.9 us
    all_to_all x2, starting transfers between devices, from_column(): lax.all_to_all(expert_sum[0].astype(jnp.bfloat16), 'expert', split_axis=0...  10.9 us
    dot_general x1, matrix products, on_device(): jnp.einsum('abjcf,abjcd->jfd', hidden, grad_column, preferred_element_typ...  10.1 us
  transfers between devices with their start and end apart: 11, of which 8 were waited for; matrix products, arithmetic and copies ran while one was open for 26% of the time, Pallas kernels for 0%

commit v1 on v0

v1 whole, which is shorter than its diff:
```python
import functools

import jax
import jax.numpy as jnp
import numpy as np
from jax import lax
from jax.experimental import pallas as pl
from jax.experimental.pallas import tpu as pltpu
from jax.sharding import PartitionSpec as P

MESH = pl.DeviceIdType.MESH
F32 = jnp.float32
BF16 = jnp.bfloat16
GELU_C = float(np.sqrt(2.0 / np.pi))


def mm(left, right, left_dim=1, right_dim=0):
    return lax.dot_general(
        left, right, (((left_dim,), (right_dim,)), ((), ())), preferred_element_type=F32
    )


def gelu_parts(v):
    square = v * v
    t = jnp.tanh(GELU_C * (v + 0.044715 * (square * v)))
    half = 0.5 * (1.0 + t)
    slope = half + (0.5 * v) * (1.0 - t * t) * (GELU_C * (1.0 + (3 * 0.044715) * square))
    return v * half, slope


def tile_of(size, want):
    while size % want:
        want //= 2
    return want


def tiles(size, want, body):
    step = tile_of(size, want)

    def one(i, carry):
        body(pl.ds(pl.multiple_of(i * step, step), step))
        return carry

    lax.fori_loop(0, size // step, one, 0)


def greet(dp_count, host_count):
    dp, ex = lax.axis_index("dp"), lax.axis_index("expert")
    barrier = pltpu.get_barrier_semaphore()
    for k in range(1, dp_count):
        pl.semaphore_signal(
            barrier, inc=1, device_id=(lax.rem(dp + k, dp_count), ex), device_id_type=MESH
        )
    for k in range(1, host_count):
        pl.semaphore_signal(
            barrier, inc=1, device_id=(dp, lax.rem(ex + k, host_count)), device_id_type=MESH
        )
    pl.semaphore_wait(barrier, dp_count - 1 + host_count - 1)
    return dp, ex


def gather_kernel(
    n, hosts,
    tok, cot, sendbuf, perm, rin_hbm, rout_hbm,
    column, partial, gin, gout,
    rin, rout, rows, arrived, slab, hid, gpre,
    wsem, lsem, dsend, drecv, asend, arecv, csend, crecv,
):
    w0 = pltpu.make_async_copy(rin_hbm, rin, wsem.at[0])
    w1 = pltpu.make_async_copy(rout_hbm, rout, wsem.at[1])
    w0.start()
    w1.start()
    dp, ex = greet(n, hosts)
    dense = []
    for a, src in enumerate((tok, cot)):
        for k in range(1, n):
            to = lax.rem(dp + k, n)
            c = pltpu.make_async_remote_copy(
                src_ref=src, dst_ref=rows.at[a, dp],
                send_sem=dsend.at[a, k - 1], recv_sem=drecv.at[a, k - 1],
                device_id=(to, ex), device_id_type=MESH,
            )
            c.start()
            dense.append(c)
        if a == 0:
            a2a = []
            for k in range(1, hosts):
                to = lax.rem(ex + k, hosts)
                c = pltpu.make_async_remote_copy(
                    src_ref=sendbuf.at[to], dst_ref=arrived.at[ex],
                    send_sem=asend.at[k - 1], recv_sem=arecv.at[k - 1],
                    device_id=(dp, to), device_id_type=MESH,
                )
                c.start()
                a2a.append(c)
    arrived[ex] = sendbuf[ex]
    rows[0, dp] = tok[...]
    rows[1, dp] = cot[...]
    for c in a2a:
        c.wait_recv()
    hr = arrived.shape[0] * arrived.shape[1]
    width = arrived.shape[2]

    def place(cols):
        got = arrived[:, :, cols].reshape(hr, cols.size)
        slab[:, cols] = mm(perm[...], got).astype(BF16)

    tiles(width, 512, place)
    local = pltpu.make_async_copy(slab, column.at[dp], lsem)
    local.start()
    col = []
    for k in range(1, n):
        to = lax.rem(dp + k, n)
        c = pltpu.make_async_remote_copy(
            src_ref=slab, dst_ref=column.at[dp],
            send_sem=csend.at[k - 1], recv_sem=crecv.at[k - 1],
            device_id=(to, ex), device_id_type=MESH,
        )
        c.start()
        col.append(c)
    w0.wait()
    w1.wait()
    for c in dense:
        c.wait_recv()
    tokens_all = n * tok.shape[0]
    hidden = rin.shape[1]

    def units(f):
        x = rows[0].reshape(tokens_all, width)
        g = rows[1].reshape(tokens_all, width)
        value, slope = gelu_parts(mm(x, rin[:, f]))
        h = value.astype(BF16)
        hid[:, f] = h
        p = (slope * mm(g, rout[f, :], 1, 1)).astype(BF16)
        gpre[:, f] = p
        gout[f, :] = mm(h, g, 0, 0).astype(BF16)
        gin[:, f] = mm(x, p, 0, 0).astype(BF16)

    tiles(hidden, 256, units)

    def back(d):
        o = mm(hid[...], rout[:, d]).astype(BF16)
        partial[0, :, :, d] = o.reshape(n, tok.shape[0], d.size)
        o = mm(gpre[...], rin[d, :], 1, 1).astype(BF16)
        partial[1, :, :, d] = o.reshape(n, tok.shape[0], d.size)

    tiles(width, 256, back)
    local.wait()
    for c in col:
        c.wait()
    for c in dense + a2a:
        c.wait_send()


def expert_kernel(
    n, hosts, local_count,
    cot, gate, kept, pick, unperm, partial, column, win_hbm, wout_hbm,
    output, grad_tokens, grad_gate, hid_out, gpre_out,
    win, wout, colv, hid, gpre, part, drecv_buf, own_dense, erecv_buf, sendback, back,
    wsem, csem, osem, dsend, drecv, esend, erecv, bsend, brecv, hsem,
):
    loads = []
    for j in range(local_count):
        c0 = pltpu.make_async_copy(win_hbm.at[j], win.at[j], wsem.at[j, 0])
        c1 = pltpu.make_async_copy(wout_hbm.at[j], wout.at[j], wsem.at[j, 1])
        cs = [
            pltpu.make_async_copy(column.at[:, a * local_count + j], colv.at[a, j], csem.at[j, a])
            for a in range(2)
        ]
        for c in [cs[0], c0, cs[1], c1]:
            c.start()
        loads.append([c0, c1] + cs)
    dp, ex = greet(n, hosts)
    dense = []
    for a in range(2):
        for k in range(1, n):
            to = lax.rem(dp + k, n)
            c = pltpu.make_async_remote_copy(
                src_ref=partial.at[a, to], dst_ref=drecv_buf.at[a, k - 1],
                send_sem=dsend.at[a, k - 1], recv_sem=drecv.at[a, k - 1],
                device_id=(to, ex), device_id_type=MESH,
            )
            c.start()
            dense.append(c)
    own = pltpu.make_async_copy(partial.at[:, dp], own_dense, osem)
    own.start()
    slots, width = colv.shape[3], colv.shape[4]
    all_rows = n * slots
    units = win.shape[2]
    scatter = [[], []]
    saves = []

    def push(a, j):
        for k in range(1, n):
            to = lax.rem(dp + k, n)
            c = pltpu.make_async_remote_copy(
                src_ref=part.at[a, j, to], dst_ref=erecv_buf.at[a, j, k - 1],
                send_sem=esend.at[a, j, k - 1], recv_sem=erecv.at[a, j, k - 1],
                device_id=(to, ex), device_id_type=MESH,
            )
            c.start()
            scatter[a].append(c)

    for j in range(local_count):
        for c in loads[j]:
            c.wait()

        def forward(f):
            x = colv[0, j].reshape(all_rows, width)
            g = colv[1, j].reshape(all_rows, width)
            value, slope = gelu_parts(mm(x, win[j, :, f]))
            hid[j, :, f] = value.astype(BF16)
            gpre[j, :, f] = (slope * mm(g, wout[j, f, :], 1, 1)).astype(BF16)

        tiles(units, 256, forward)

        def project(d):
            o = mm(hid[j], wout[j, :, d]).astype(BF16)
            part[0, j, :, :, d] = o.reshape(n, slots, d.size)

        tiles(width, 256, project)
        push(0, j)

        def project_back(d):
            o = mm(gpre[j], win[j, d, :], 1, 1).astype(BF16)
            part[1, j, :, :, d] = o.reshape(n, slots, d.size)

        tiles(width, 256, project_back)
        push(1, j)
        for s, (src, dst) in enumerate(((hid, hid_out), (gpre, gpre_out))):
            c = pltpu.make_async_copy(src.at[j], dst.at[j], hsem.at[j, s])
            c.start()
            saves.append(c)

    back_copies = [[], []]
    hr = back.shape[1] * back.shape[2]
    for a in range(2):
        for c in scatter[a]:
            c.wait_recv()

        def collect(d):
            total = part[a, :, dp, :, d].astype(F32)
            for k in range(n - 1):
                total = total + erecv_buf[a, :, k, :, d].astype(F32)
            summed = total.astype(BF16).reshape(local_count * slots, d.size)
            o = mm(unperm[...], summed).astype(BF16)
            sendback[a, :, :, d] = o.reshape(back.shape[1], back.shape[2], d.size)

        tiles(width, 256, collect)
        for k in range(1, hosts):
            to = lax.rem(ex + k, hosts)
            c = pltpu.make_async_remote_copy(
                src_ref=sendback.at[a, to], dst_ref=back.at[a, ex],
                send_sem=bsend.at[a, k - 1], recv_sem=brecv.at[a, k - 1],
                device_id=(dp, to), device_id_type=MESH,
            )
            c.start()
            back_copies[a].append(c)
        back[a, ex] = sendback[a, ex]
    own.wait()
    for c in dense:
        c.wait_recv()

    for a in range(2):
        for c in back_copies[a]:
            c.wait_recv()

        for lo in range(0, width, tile_of(width, 512)):
            d = pl.ds(lo, tile_of(width, 512))
            total = own_dense[a, :, d].astype(F32)
            for k in range(n - 1):
                total = total + drecv_buf[a, k, :, d].astype(F32)
            mine = mm(pick[...], back[a, :, :, d].reshape(hr, d.size))
            if a == 0:
                output[:, d] = (total + gate[...] * mine).astype(BF16)
                term = jnp.sum(cot[:, d].astype(F32) * mine, axis=1, keepdims=True)
                gg = term if lo == 0 else gg + term
            else:
                grad_tokens[:, d] = (total + mine).astype(BF16)
        if a == 0:
            grad_gate[...] = kept[...] * gg
    for c in saves:
        c.wait()
    for c in dense + scatter[0] + scatter[1] + back_copies[0] + back_copies[1]:
        c.wait_send()


def ceil16(v):
    return -(-v // 16) * 16


def on_device(
    tokens, gate_prob, expert_index, slot_index, dropped, cotangent,
    expert_in, expert_out, residual_in, residual_out,
):
    n = lax.axis_size("dp")
    hosts = lax.axis_size("expert")
    local_count, width, units = expert_in.shape
    hidden = residual_in.shape[1]
    experts_all = local_count * hosts
    row_count = tokens.shape[0]
    capacity = max(2, 5 * row_count // (4 * experts_all))
    kept = (dropped == 0) & (slot_index < capacity)
    kept_float = kept.astype(F32)
    gate_kept = gate_prob * kept_float
    block = local_count * capacity
    send_rows = ceil16(2 * block)
    back_rows = ceil16(block)
    slots = ceil16(hosts * capacity)

    host = expert_index // local_count
    within = (expert_index % local_count) * capacity + slot_index
    send_pos = jnp.where(kept, host * send_rows + within, -1)
    back_pos = jnp.where(kept, host * back_rows + within, -1)
    scaled = (cotangent.astype(F32) * gate_kept[:, None]).astype(BF16)
    target = jnp.arange(hosts * send_rows, dtype=jnp.int32)[:, None]
    grad_pos = jnp.where(kept, send_pos + block, -1)
    place = jnp.concatenate(
        [(target == send_pos[None]).astype(BF16), (target == grad_pos[None]).astype(BF16)], axis=1
    )
    sendbuf = mm(place, jnp.concatenate([tokens, scaled], axis=0)).astype(BF16)
    sendbuf = sendbuf.reshape(hosts, send_rows, width)
    pick = (jnp.arange(hosts * back_rows, dtype=jnp.int32)[None] == back_pos[:, None]).astype(BF16)

    perm = np.zeros((2, local_count, slots, hosts, send_rows), np.float32)
    unperm = np.zeros((hosts, back_rows, local_count, slots), np.float32)
    for j in range(local_count):
        for h in range(hosts):
            for c in range(capacity):
                unperm[h, j * capacity + c, j, h * capacity + c] = 1
                for a in range(2):
                    perm[a, j, h * capacity + c, h, a * block + j * capacity + c] = 1
    perm = jnp.asarray(perm.reshape(2 * local_count * slots, hosts * send_rows), BF16)
    unperm = jnp.asarray(unperm.reshape(hosts * back_rows, local_count * slots), BF16)

    vmem = pl.BlockSpec(memory_space=pltpu.VMEM)
    anyspace = pl.BlockSpec(memory_space=pl.ANY)
    dma = pltpu.SemaphoreType.DMA
    tokens_all = n * row_count
    column, partial, gin, gout = pl.pallas_call(
        functools.partial(gather_kernel, n, hosts),
        out_shape=(
            jax.ShapeDtypeStruct((n, 2 * local_count * slots, width), BF16),
            jax.ShapeDtypeStruct((2, n, row_count, width), BF16),
            jax.ShapeDtypeStruct((width, hidden), BF16),
            jax.ShapeDtypeStruct((hidden, width), BF16),
        ),
        in_specs=[vmem, vmem, vmem, vmem, anyspace, anyspace],
        out_specs=(anyspace, vmem, vmem, vmem),
        scratch_shapes=[
            pltpu.VMEM((width, hidden), BF16),
            pltpu.VMEM((hidden, width), BF16),
            pltpu.VMEM((2, n, row_count, width), BF16),
            pltpu.VMEM((hosts, send_rows, width), BF16),
            pltpu.VMEM((2 * local_count * slots, width), BF16),
            pltpu.VMEM((tokens_all, hidden), BF16),
            pltpu.VMEM((tokens_all, hidden), BF16),
            dma((2,)),
            dma,
            dma((2, n - 1)),
            dma((2, n - 1)),
            dma((hosts - 1,)),
            dma((hosts - 1,)),
            dma((n - 1,)),
            dma((n - 1,)),
        ],
        compiler_params=pltpu.CompilerParams(
            collective_id=0, has_side_effects=True, vmem_limit_bytes=56 * 2**20
        ),
        name="gather_dense",
    )(tokens, cotangent, sendbuf, perm, residual_in, residual_out)

    in_total, out_total = lax.psum((gin, gout), "expert")

    column = column.reshape(n, 2 * local_count, slots, width)
    all_rows = n * slots
    output, grad_tokens, grad_gate, hid, gpre = pl.pallas_call(
        functools.partial(expert_kernel, n, hosts, local_count),
        out_shape=(
            jax.ShapeDtypeStruct((row_count, width), BF16),
            jax.ShapeDtypeStruct((row_count, width), BF16),
            jax.ShapeDtypeStruct((row_count, 1), F32),
            jax.ShapeDtypeStruct((local_count, all_rows, units), BF16),
            jax.ShapeDtypeStruct((local_count, all_rows, units), BF16),
        ),
        in_specs=[vmem] * 5 + [anyspace] * 4,
        out_specs=(vmem, vmem, vmem, anyspace, anyspace),
        scratch_shapes=[
            pltpu.VMEM((local_count, width, units), BF16),
            pltpu.VMEM((local_count, units, width), BF16),
            pltpu.VMEM((2, local_count, n, slots, width), BF16),
            pltpu.VMEM((local_count, all_rows, units), BF16),
            pltpu.VMEM((local_count, all_rows, units), BF16),
            pltpu.VMEM((2, local_count, n, slots, width), BF16),
            pltpu.VMEM((2, n - 1, row_count, width), BF16),
            pltpu.VMEM((2, row_count, width), BF16),
            pltpu.VMEM((2, local_count, n - 1, slots, width), BF16),
            pltpu.VMEM((2, hosts, back_rows, width), BF16),
            pltpu.VMEM((2, hosts, back_rows, width), BF16),
            dma((local_count, 2)),
            dma((local_count, 2)),
            dma,
            dma((2, n - 1)),
            dma((2, n - 1)),
            dma((2, local_count, n - 1)),
            dma((2, local_count, n - 1)),
            dma((2, hosts - 1)),
            dma((2, hosts - 1)),
            dma((local_count, 2)),
        ],
        compiler_params=pltpu.CompilerParams(
            collective_id=1, has_side_effects=True, vmem_limit_bytes=60 * 2**20
        ),
        name="expert_scatter",
    )(
        cotangent, gate_kept[:, None], kept_float[:, None], pick, unperm,
        partial, column, expert_in, expert_out,
    )

    grad_expert_out = jnp.einsum(
        "jnsf,njsd->jfd", hid.reshape(local_count, n, slots, units), column[:, local_count:],
        preferred_element_type=F32,
    ).astype(BF16)
    grad_expert_in = jnp.einsum(
        "njsd,jnsf->jdf", column[:, :local_count], gpre.reshape(local_count, n, slots, units),
        preferred_element_type=F32,
    ).astype(BF16)
    return (
        output,
        grad_tokens,
        grad_gate[:, 0],
        grad_expert_in,
        grad_expert_out,
        in_total,
        out_total,
    )


def solution(mesh):
    return jax.shard_map(
        on_device,
        mesh=mesh,
        in_specs=(
            P(("dp", "expert"), None),
            P(("dp", "expert")),
            P(("dp", "expert")),
            P(("dp", "expert")),
            P(("dp", "expert")),
            P(("dp", "expert"), None),
            P("expert", None, "dp"),
            P("expert", "dp", None),
            P(None, "dp"),
            P("dp", None),
        ),
        out_specs=(
            P(("dp", "expert"), None),
            P(("dp", "expert"), None),
            P(("dp", "expert")),
            P("expert", None, "dp"),
            P("expert", "dp", None),
            P(None, "dp"),
            P("dp", None),
        ),
        check_vma=False,
    )
```

time: 442 us -> 265 us (0.60)
  waiting for transfers between devices: 253 us -> 0.02 us
  Pallas kernels: 0 us -> 214 us
  matrix products: 83.8 us -> 24.1 us
  blocking collectives: 35.1 us -> 0 us
  local copies, waits for them, and re-layouts: 34.8 us -> 7.77 us
  starting transfers between devices: 11.7 us -> 0.04 us
    pallas_call x0 -> x2, Pallas kernels: none -> 214 us  [the longest x1 128 us: on_device(): pl.pallas_call(functools.partial(expert_kernel, n, hosts, local_count), o...]
    psum x1, waiting for transfers between devices: 101 us -> 0.01 us  [on_device(): in_total, out_total = lax.psum((gin, gout), 'expert')]
    unnamed x13 -> x1, waiting for transfers between devices: 96.1 us -> 0.02 us
    dot_general x12 -> x3, matrix products: 83.8 us -> 24.1 us  [the longest x1 12.1 us: on_device(): jnp.einsum('njsd,jnsf->jdf', column[:, :local_count], gpre.reshape(local_...]
    all_gather x4 -> x0, waiting for transfers between devices: 55.7 us -> none  [the longest x2 34.7 us: to_column(): lax.all_gather(arrived[None], 'dp', axis=0, tiled=True)]
    all_to_all x2 -> x0, blocking collectives: 35.1 us -> none  [to_column(): lax.all_to_all(own_buffer, 'expert', split_axis=0, concat_axis=0, tiled=T...]
    all_to_all x2 -> x0, starting transfers between devices: 10.9 us -> none  [from_column(): lax.all_to_all(expert_sum[0].astype(jnp.bfloat16), 'expert', split_axis=0...]
    convert_element_type x4 -> x0, local copies, waits for them, and re-layouts: 9.48 us -> none  [the longest x2 4.84 us: from_column(): expert_part.astype(jnp.bfloat16)]
  transfers between devices with their start and end apart: 11 -> 1, of which waited for: 8 -> 0; matrix products, arithmetic and copies ran while one was open for 26% -> 10% of each run, Pallas kernels for 0% -> 48%
where the time goes in v1:
time: 265 us
  Pallas kernels  214 us (81%)
  matrix products  24.1 us (9%)
  between operations  14.1 us (5%)
  local copies, waits for them, and re-layouts  7.77 us (3%)
  other arithmetic  4.75 us (2%)
    pallas_call x1, Pallas kernels, on_device(): pl.pallas_call(functools.partial(expert_kernel, n, hosts, local_count), o...  128 us
    pallas_call x1, Pallas kernels, on_device(): pl.pallas_call(functools.partial(gather_kernel, n, hosts), out_shape=(jax...  86 us
    dot_general x1, matrix products, on_device(): jnp.einsum('njsd,jnsf->jdf', column[:, :local_count], gpre.reshape(local_...  12.1 us
    dot_general x1, matrix products, on_device(): jnp.einsum('jnsf,njsd->jfd', hid.reshape(local_count, n, slots, units), c...  9.55 us
    unnamed x14, local copies, waits for them, and re-layouts  6.29 us
  transfers between devices with their start and end apart: 1, of which 0 were waited for; matrix products, arithmetic and copies ran while one was open for 10% of the time, Pallas kernels for 48%

profile of v1, /device:TPU:9, one launch (start us, length us, event | category | flops | bytes accessed | tf_op | source)
XLA Modules:
  0.0 264.9 jit_solution(15224753005345586938)
XLA Ops:
  7.2 0.0 all-reduce.3.cloned.1.call-start
  7.2 0.7 add_select_fusion
  7.9 0.7 broadcast_select_fusion
  8.6 0.1 iota_compare_fusion
  8.6 1.1 multiply_convert_fusion
  9.8 2.5 convolution_convert_fusion
  12.3 86.0 %gather_dense.1 = (bf16[4,320,1536]{2,1,0:T(8,128)(2,1)}, bf16[2,4,128,1536]{3,2,1,0:T(8,128)(2,1)}, bf16[1536,768]{1,0:T(8,128)(2,1)}, bf16[768,1536]{1,0:T(8,128)(2,1)}) custom-call(bf16[128,1536]{1,0:T(8,128)(2,1)} %tok.1, bf16[128,1536]{1,0:T(8,128)(2,1)} %cot.3, bf16[8,48,1536]{2,1,0:T(8,128)(2,1)} %bitcast.17, bf16[320,384]{1,0:T(8,128)(2,1)} %constant.42.clone.perm, ...), custom_call_target="tpu_custom_call" | custom-call | tf_op jit(solution)/shard_map/gather_dense/pallas_call | solution.py:340
  98.3 0.0 all-reduce.3.cloned.1.call-update
  98.3 0.7 copy.24.kept
  99.0 0.7 fusion.8.pick
  99.8 0.7 copy.23.gate
  100.5 128.1 %expert_scatter.1 = (bf16[128,1536]{1,0:T(8,128)(2,1)}, bf16[128,1536]{1,0:T(8,128)(2,1)}, f32[128,1]{1,0:T(8,128)}, bf16[2,320,1536]{2,1,0:T(8,128)(2,1)}, bf16[2,320,1536]{2,1,0:T(8,128)(2,1)}) custom-call(bf16[128,1536]{1,0:T(8,128)(2,1)} %cot.3, f32[128,1]{1,0:T(8,128)} %copy.23.gate, f32[128,1]{1,0:T(8,128)} %copy.24.kept, ...), custom_call_target="tpu_custom_call" | custom-call | tf_op jit(solution)/shard_map/expert_scatter/pallas_call | solution.py:377
  228.6 1.5 reduce
  230.1 9.5 %bitcast_convert_fusion = bf16[2,1536,1536]{2,1,0:T(8,128)(2,1)} fusion(bf16[2,4,80,1536]{3,2,1,0:T(8,128)(2,1)} %bitcast.20, bf16[4,4,80,1536]{3,2,1,0:T(8,128)(2,1)} %bitcast.15), kind=kOutput, calls=%fused_computation | convolution fusion | flops 3024617472 | bytes 13369344 | tf_op jit(solution)/shard_map/jnsf,njsd->jfd/dot_general | solution.py:420
  239.6 0.0 copy-done
  239.6 0.0 copy-done.4
  239.7 0.0 copy-start.2
  239.7 12.1 %bitcast_convert_fusion.1 = bf16[2,1536,1536]{2,1,0:T(8,128)(2,1)} fusion(bf16[4,4,80,1536]{3,2,1,0:T(8,128)(2,1)S(1)} %bitcast.16, bf16[2,4,80,1536]{3,2,1,0:T(8,128)(2,1)S(1)} %bitcast.19), kind=kOutput, calls=%fused_computation.1 | convolution fusion | flops 3024617472 | bytes 15335424 | tf_op jit(solution)/shard_map/njsd,jnsf->jdf/dot_general | solution.py:424
  251.8 0.0 copy-done.3
  251.8 0.7 copy.44
  252.5 0.0 copy-done.2
  252.5 0.7 copy.45
  253.3 3.4 %copy.46 = bf16[1536,768]{1,0:T(8,128)(2,1)} copy(bf16[1536,768]{1,0:T(8,128)(2,1)} %get-tuple-element.46) | data formatting | bytes 4718592
  256.6 1.4 copy.47
  (8 shorter events, 0.0 us)
Async XLA Ops:
  7.2 244.6 %all-reduce.3.cloned.1.call-start = ((), (), s32[]{:S(2)}) async-start(), calls=%async_computation | async-start | bytes 9437184 | tf_op jit(solution)/shard_map/psum | solution.py:373
  230.1 9.6 %copy-start = (bf16[4,320,1536]{2,1,0:T(8,128)(2,1)S(1)}, bf16[4,320,1536]{2,1,0:T(8,128)(2,1)}, u32[]{:S(2)}) copy-start(bf16[4,320,1536]{2,1,0:T(8,128)(2,1)} %get-tuple-element.17) | copy-start | bytes 11796484
  230.1 9.6 %copy-start.4 = (bf16[2,320,1536]{2,1,0:T(8,128)(2,1)S(1)}, bf16[2,320,1536]{2,1,0:T(8,128)(2,1)}, u32[]{:S(2)}) copy-start(bf16[2,320,1536]{2,1,0:T(8,128)(2,1)} %get-tuple-element.21) | copy-start | bytes 5898244
  239.6 12.1 %copy-start.3 = (bf16[128,1536]{1,0:T(8,128)(2,1)S(1)}, bf16[128,1536]{1,0:T(8,128)(2,1)}, u32[]{:S(2)}) copy-start(bf16[128,1536]{1,0:T(8,128)(2,1)} %get-tuple-element.41) | copy-start | bytes 1179652
  239.7 12.9 %copy-start.2 = (bf16[128,1536]{1,0:T(8,128)(2,1)S(1)}, bf16[128,1536]{1,0:T(8,128)(2,1)}, u32[]{:S(2)}) copy-start(bf16[128,1536]{1,0:T(8,128)(2,1)} %get-tuple-element.42) | copy-start | bytes 1179652
  253.3 3.4 %copy-start.1 = (bf16[768,1536]{1,0:T(8,128)(2,1)S(1)}, bf16[768,1536]{1,0:T(8,128)(2,1)}, u32[]{:S(2)}) copy-start(bf16[768,1536]{1,0:T(8,128)(2,1)} %get-tuple-element.47) | copy-start | bytes 7077892
Sparse Core Ops, SparseCore 0:
  98.4 139.9 all-reduce.2

commit v2 on v1

v2 whole, which is shorter than its diff:
```python
import functools

import jax
import jax.numpy as jnp
import numpy as np
from jax import lax
from jax.experimental import pallas as pl
from jax.experimental.pallas import tpu as pltpu
from jax.sharding import PartitionSpec as P

MESH = pl.DeviceIdType.MESH
F32 = jnp.float32
BF16 = jnp.bfloat16
GELU_C = float(np.sqrt(2.0 / np.pi))


def mm(left, right, left_dim=1, right_dim=0):
    return lax.dot_general(
        left, right, (((left_dim,), (right_dim,)), ((), ())), preferred_element_type=F32
    )


def gelu_parts(v):
    square = v * v
    t = jnp.tanh(GELU_C * (v + 0.044715 * (square * v)))
    half = 0.5 * (1.0 + t)
    slope = half + (0.5 * v) * (1.0 - t * t) * (GELU_C * (1.0 + (3 * 0.044715) * square))
    return v * half, slope


def tile_of(size, want):
    while size % want:
        want //= 2
    return want


def tiles(size, want, body):
    step = tile_of(size, want)

    def one(i, carry):
        body(pl.ds(pl.multiple_of(i * step, step), step))
        return carry

    lax.fori_loop(0, size // step, one, 0)


def greet(dp_count, host_count):
    dp, ex = lax.axis_index("dp"), lax.axis_index("expert")
    barrier = pltpu.get_barrier_semaphore()
    for k in range(1, dp_count):
        pl.semaphore_signal(
            barrier, inc=1, device_id=(lax.rem(dp + k, dp_count), ex), device_id_type=MESH
        )
    for k in range(1, host_count):
        pl.semaphore_signal(
            barrier, inc=1, device_id=(dp, lax.rem(ex + k, host_count)), device_id_type=MESH
        )
    pl.semaphore_wait(barrier, dp_count - 1 + host_count - 1)
    return dp, ex


def layer_kernel(
    n, hosts, local_count, reduce_here,
    tok, cot, sendbuf, perm, gate, kept, pick, unperm, rin_hbm, rout_hbm, win_hbm, wout_hbm,
    output, grad_tokens, grad_gate, gin, gout, gwin, gwout,
    rin, rout, rows, arrived, colv, dhid, dgpre, partial, pin, pout, in1, out1, in2, out2,
    win, wout, hid, gpre, part, drecv_buf, erecv_buf, back,
    wsem, gsem, asend, arecv, bsend, brecv, hsend, hrecv, dsend, drecv, esend, erecv,
    csend, crecv, psend, precv, qsend, qrecv, ssend, srecv, lsem,
):
    loads = [pltpu.make_async_copy(rin_hbm, rin, wsem.at[0, 0]),
             pltpu.make_async_copy(rout_hbm, rout, wsem.at[0, 1])]
    for j in range(local_count):
        loads.append(pltpu.make_async_copy(win_hbm.at[j], win.at[j], wsem.at[1 + j, 0]))
        loads.append(pltpu.make_async_copy(wout_hbm.at[j], wout.at[j], wsem.at[1 + j, 1]))
    for c in loads:
        c.start()
    dp, ex = greet(n, hosts)
    sends = []

    def remote(src, dst, send_sem, recv_sem, to):
        c = pltpu.make_async_remote_copy(
            src_ref=src, dst_ref=dst, send_sem=send_sem, recv_sem=recv_sem,
            device_id=to, device_id_type=MESH,
        )
        c.start()
        sends.append(c)
        return c

    square = n == 4
    beside = lax.div(dp, 2) * 2 + 1 - lax.rem(dp, 2) if square else None
    across = lax.rem(dp + 2, n) if square else None

    def spread(srcs, buf, ssem, rsem):
        if not square:
            return [
                [remote(srcs[a], buf.at[a, dp], ssem.at[a, k - 1], rsem.at[a, k - 1],
                        (lax.rem(dp + k, n), ex)) for k in range(1, n)]
                for a in range(2)
            ]
        return [
            [remote(srcs[a], buf.at[a, dp], ssem.at[a, k], rsem.at[a, k], (to, ex))
             for k, to in enumerate((beside, across))]
            for a in range(2)
        ]

    def relay(copies, buf, ssem, rsem):
        if not square:
            return [c for pair in copies for c in pair]
        copies[0][1].wait_recv()
        f0 = remote(buf.at[0, across], buf.at[0, across], ssem.at[0, 2], rsem.at[0, 2], (beside, ex))
        copies[1][0].wait_recv()
        f1 = remote(buf.at[1, beside], buf.at[1, beside], ssem.at[1, 2], rsem.at[1, 2], (across, ex))
        return [copies[0][0], copies[1][1], f0, f1]

    row_count, width = tok.shape
    tokens_all = n * row_count
    hidden = rin.shape[1]
    rows[0, dp] = tok[...]
    rows[1, dp] = cot[...]
    dense = spread((tok, cot), rows, asend, arecv)
    a2a = [
        remote(sendbuf.at[to], arrived.at[ex], bsend.at[k - 1], brecv.at[k - 1], (dp, to))
        for k, to in ((k, lax.rem(ex + k, hosts)) for k in range(1, hosts))
    ]
    keep = pltpu.make_async_copy(sendbuf.at[ex], arrived.at[ex], lsem.at[2])
    keep.start()
    rest = relay(dense, rows, asend, arecv)
    mark = len(sends)
    for c in a2a:
        c.wait_recv()
    keep.wait()
    hr = arrived.shape[0] * arrived.shape[1]
    slots = colv.shape[3]

    def place(cols):
        got = arrived[:, :, cols].reshape(hr, cols.size)
        put = mm(perm[...], got).astype(BF16)
        colv[:, dp, :, :, cols] = put.reshape(2, local_count, slots, cols.size)

    tiles(width, 512, place)
    column = spread((colv.at[0, dp], colv.at[1, dp]), colv, hsend, hrecv)
    loads[0].wait()
    loads[1].wait()
    for c in rest:
        c.wait_recv()

    def dense_units(f):
        x = rows[0].reshape(tokens_all, width)
        g = rows[1].reshape(tokens_all, width)
        value, slope = gelu_parts(mm(x, rin[:, f]))
        h = value.astype(BF16)
        dhid[:, f] = h
        p = (slope * mm(g, rout[f, :], 1, 1)).astype(BF16)
        dgpre[:, f] = p
        pout[f, :] = mm(h, g, 0, 0).astype(BF16)
        pin[:, f] = mm(x, p, 0, 0).astype(BF16)

    tiles(hidden, 256, dense_units)

    chips = hosts // 2
    chip, core = lax.div(ex, 2), lax.rem(ex, 2)
    other = 1 - core
    sibling = chip * 2 + other
    pairs = ((pin, in1, in2, rin, gin), (pout, out1, out2, rout, gout))

    def block_of(ref, c, q):
        size = ref.shape[0] // hosts
        return pl.ds(pl.multiple_of((c * chips + q) * size, 16), size)

    def half_of(ref, c):
        size = ref.shape[0] // 2
        return pl.ds(pl.multiple_of(c * size, 16), size)

    if reduce_here:
        first = [
            remote(p.at[half_of(p, other)], r1, psend.at[i], precv.at[i], (dp, sibling))
            for i, (p, r1, r2, s, o) in enumerate(pairs)
        ]

    def dense_back(d):
        o = mm(dhid[...], rout[:, d]).astype(BF16)
        partial[0, :, :, d] = o.reshape(n, row_count, d.size)
        o = mm(dgpre[...], rin[d, :], 1, 1).astype(BF16)
        partial[1, :, :, d] = o.reshape(n, row_count, d.size)

    tiles(width, 256, dense_back)
    second = []
    if reduce_here:
        for i, (p, r1, r2, s, o) in enumerate(pairs):
            first[i].wait_recv()
            size = p.shape[0] // hosts
            for q in range(chips):
                at = pl.ds(q * size, size)
                s[at, :] = (p[block_of(p, core, q), :].astype(F32) + r1[at, :].astype(F32)).astype(BF16)
            for k in range(1, chips):
                q = lax.rem(chip + k, chips)
                second.append(remote(
                    s.at[pl.ds(pl.multiple_of(q * size, 16), size)], r2.at[k - 1],
                    psend.at[2 + i * (chips - 1) + k - 1], precv.at[2 + i * (chips - 1) + k - 1],
                    (dp, q * 2 + core),
                ))
    else:
        saves = [pltpu.make_async_copy(pin, gin, lsem.at[0]), pltpu.make_async_copy(pout, gout, lsem.at[1])]
        for c in saves:
            c.start()
    rest = relay(column, colv, hsend, hrecv)
    dense_rs = [
        remote(partial.at[a, to], drecv_buf.at[a, k - 1], dsend.at[a, k - 1], drecv.at[a, k - 1], (to, ex))
        for a in range(2) for k, to in ((k, lax.rem(dp + k, n)) for k in range(1, n))
    ]
    for c in rest:
        c.wait_recv()

    all_rows = n * slots
    units = win.shape[2]
    scatter = [[], []]

    def push(a, j):
        for k in range(1, n):
            to = lax.rem(dp + k, n)
            scatter[a].append(remote(
                part.at[a, j, to], erecv_buf.at[a, j, k - 1],
                esend.at[a, j, k - 1], erecv.at[a, j, k - 1], (to, ex),
            ))

    for j in range(local_count):
        loads[2 + 2 * j].wait()
        loads[3 + 2 * j].wait()

        def forward(f):
            x = colv[0, :, j].reshape(all_rows, width)
            g = colv[1, :, j].reshape(all_rows, width)
            value, slope = gelu_parts(mm(x, win[j, :, f]))
            hid[j, :, f] = value.astype(BF16)
            gpre[j, :, f] = (slope * mm(g, wout[j, f, :], 1, 1)).astype(BF16)

        tiles(units, 256, forward)

        def project(d):
            o = mm(hid[j], wout[j, :, d]).astype(BF16)
            part[0, j, :, :, d] = o.reshape(n, slots, d.size)

        tiles(width, 256, project)
        push(0, j)

        def project_back(d):
            o = mm(gpre[j], win[j, d, :], 1, 1).astype(BF16)
            part[1, j, :, :, d] = o.reshape(n, slots, d.size)

        tiles(width, 256, project_back)
        push(1, j)

    third = []
    if reduce_here:
        saves = []
        for c in second:
            c.wait_recv()
        for i, (p, r1, r2, s, o) in enumerate(pairs):
            size = p.shape[0] // hosts
            total = s[pl.ds(pl.multiple_of(chip * size, 16), size), :].astype(F32)
            for k in range(chips - 1):
                total = total + r2[k].astype(F32)
            done = s.at[pl.ds(chips * size, size)]
            done[...] = total.astype(BF16)
            c = pltpu.make_async_copy(done, o.at[block_of(o, core, chip)], lsem.at[i])
            c.start()
            saves.append(c)
            for k in range(1, chips):
                q = lax.rem(chip + k, chips)
                third.append(remote(
                    done, o.at[block_of(o, core, chip)],
                    qsend.at[i, k - 1], qrecv.at[i, k - 1], (dp, q * 2 + core),
                ))

    grads = []
    for j in range(local_count):

        def weights(f):
            g = colv[1, :, j].reshape(all_rows, width)
            wout[j, f, :] = mm(hid[j, :, f], g, 0, 0).astype(BF16)
            x = colv[0, :, j].reshape(all_rows, width)
            win[j, :, f] = mm(x, gpre[j, :, f], 0, 0).astype(BF16)

        tiles(units, 256, weights)
        for s, (src, dst) in enumerate(((win, gwin), (wout, gwout))):
            c = pltpu.make_async_copy(src.at[j], dst.at[j], gsem.at[j, s])
            c.start()
            grads.append(c)

    back_rows = back.shape[2]
    back_all = hosts * back_rows
    back_copies = [[], []]
    per = row_count // back_rows

    def rows_for(a, host):
        start = pl.multiple_of(lax.rem(host, per) * back_rows, back_rows)
        return rows.at[a, lax.div(host, per), pl.ds(start, back_rows)]

    for c in sends[:mark]:
        c.wait_send()
    for a in range(2):
        for c in scatter[a]:
            c.wait_recv()

        def collect(d):
            total = part[a, :, dp, :, d].astype(F32)
            for k in range(n - 1):
                total = total + erecv_buf[a, :, k, :, d].astype(F32)
            summed = total.astype(BF16).reshape(local_count * slots, d.size)
            o = mm(unperm[...], summed).astype(BF16)
            rows[a, :hosts // per, :, d] = o.reshape(hosts // per, row_count, d.size)

        tiles(width, 256, collect)
        for k in range(1, hosts):
            to = lax.rem(ex + k, hosts)
            back_copies[a].append(remote(
                rows_for(a, to), back.at[a, ex], csend.at[a, k - 1], crecv.at[a, k - 1], (dp, to)
            ))
        back[a, ex] = rows_for(a, ex)[...]
    fourth = []
    if reduce_here:
        for c in saves:
            c.wait()
        for c in third:
            c.wait_recv()
        for i, (p, r1, r2, s, o) in enumerate(pairs):
            fourth.append(remote(
                o.at[half_of(o, core)], o.at[half_of(o, core)], ssend.at[i], srecv.at[i], (dp, sibling)
            ))
        saves = []
    for c in dense_rs:
        c.wait_recv()

    for a in range(2):
        for c in back_copies[a]:
            c.wait_recv()
        for lo in range(0, width, tile_of(width, 512)):
            d = pl.ds(lo, tile_of(width, 512))
            total = partial[a, dp, :, d].astype(F32)
            for k in range(n - 1):
                total = total + drecv_buf[a, k, :, d].astype(F32)
            mine = mm(pick[...], back[a, :, :, d].reshape(back_all, d.size))
            if a == 0:
                output[:, d] = (total + gate[...] * mine).astype(BF16)
                term = jnp.sum(cot[:, d].astype(F32) * mine, axis=1, keepdims=True)
                gg = term if lo == 0 else gg + term
            else:
                grad_tokens[:, d] = (total + mine).astype(BF16)
        if a == 0:
            grad_gate[...] = kept[...] * gg
    for c in grads + saves:
        c.wait()
    for c in fourth:
        c.wait_recv()
    for c in sends[mark:]:
        c.wait_send()


def ceil16(v):
    return -(-v // 16) * 16


def on_device(
    tokens, gate_prob, expert_index, slot_index, dropped, cotangent,
    expert_in, expert_out, residual_in, residual_out,
):
    n = lax.axis_size("dp")
    hosts = lax.axis_size("expert")
    local_count, width, units = expert_in.shape
    hidden = residual_in.shape[1]
    experts_all = local_count * hosts
    row_count = tokens.shape[0]
    capacity = max(2, 5 * row_count // (4 * experts_all))
    kept = (dropped == 0) & (slot_index < capacity)
    kept_float = kept.astype(F32)
    gate_kept = gate_prob * kept_float
    block = local_count * capacity
    send_rows = ceil16(2 * block)
    back_rows = ceil16(block)
    slots = ceil16(hosts * capacity)

    host = expert_index // local_count
    within = (expert_index % local_count) * capacity + slot_index
    send_pos = jnp.where(kept, host * send_rows + within, -1)
    back_pos = jnp.where(kept, host * back_rows + within, -1)
    scaled = (cotangent.astype(F32) * gate_kept[:, None]).astype(BF16)
    target = jnp.arange(hosts * send_rows, dtype=jnp.int32)[:, None]
    grad_pos = jnp.where(kept, send_pos + block, -1)
    place = jnp.concatenate(
        [(target == send_pos[None]).astype(BF16), (target == grad_pos[None]).astype(BF16)], axis=1
    )
    sendbuf = mm(place, jnp.concatenate([tokens, scaled], axis=0)).astype(BF16)
    sendbuf = sendbuf.reshape(hosts, send_rows, width)
    pick = (jnp.arange(hosts * back_rows, dtype=jnp.int32)[None] == back_pos[:, None]).astype(BF16)

    perm = np.zeros((2, local_count, slots, hosts, send_rows), np.float32)
    unperm = np.zeros((hosts, back_rows, local_count, slots), np.float32)
    for j in range(local_count):
        for h in range(hosts):
            for c in range(capacity):
                unperm[h, j * capacity + c, j, h * capacity + c] = 1
                for a in range(2):
                    perm[a, j, h * capacity + c, h, a * block + j * capacity + c] = 1
    perm = jnp.asarray(perm.reshape(2 * local_count * slots, hosts * send_rows), BF16)
    unperm = jnp.asarray(unperm.reshape(hosts * back_rows, local_count * slots), BF16)

    vmem = pl.BlockSpec(memory_space=pltpu.VMEM)
    anyspace = pl.BlockSpec(memory_space=pl.ANY)
    dma = pltpu.SemaphoreType.DMA
    all_rows = n * slots
    reduce_here = hosts % 2 == 0 and width % (16 * hosts) == 0 and hidden % (16 * hosts) == 0
    chips = hosts // 2
    reduce_shapes = (
        (width // 2, hidden),
        (hidden // 2, width),
        (chips - 1, width // hosts, hidden),
        (chips - 1, hidden // hosts, width),
    )
    output, grad_tokens, grad_gate, in_total, out_total, grad_expert_in, grad_expert_out = pl.pallas_call(
        functools.partial(layer_kernel, n, hosts, local_count, reduce_here),
        out_shape=(
            jax.ShapeDtypeStruct((row_count, width), BF16),
            jax.ShapeDtypeStruct((row_count, width), BF16),
            jax.ShapeDtypeStruct((row_count, 1), F32),
            jax.ShapeDtypeStruct((width, hidden), BF16),
            jax.ShapeDtypeStruct((hidden, width), BF16),
            jax.ShapeDtypeStruct((local_count, width, units), BF16),
            jax.ShapeDtypeStruct((local_count, units, width), BF16),
        ),
        in_specs=[vmem] * 2 + [anyspace] + [vmem] * 5 + [anyspace] * 4,
        out_specs=(vmem, vmem, vmem, anyspace, anyspace, anyspace, anyspace),
        scratch_shapes=[
            pltpu.VMEM((width, hidden), BF16),
            pltpu.VMEM((hidden, width), BF16),
            pltpu.VMEM((2, n, row_count, width), BF16),
            pltpu.VMEM((hosts, send_rows, width), BF16),
            pltpu.VMEM((2, n, local_count, slots, width), BF16),
            pltpu.VMEM((n * row_count, hidden), BF16),
            pltpu.VMEM((n * row_count, hidden), BF16),
            pltpu.VMEM((2, n, row_count, width), BF16),
            pltpu.VMEM((width, hidden), BF16),
            pltpu.VMEM((hidden, width), BF16),
            *(pltpu.VMEM(shape if reduce_here else (16, 128), BF16) for shape in reduce_shapes),
            pltpu.VMEM((local_count, width, units), BF16),
            pltpu.VMEM((local_count, units, width), BF16),
            pltpu.VMEM((local_count, all_rows, units), BF16),
            pltpu.VMEM((local_count, all_rows, units), BF16),
            pltpu.VMEM((2, local_count, n, slots, width), BF16),
            pltpu.VMEM((2, n - 1, row_count, width), BF16),
            pltpu.VMEM((2, local_count, n - 1, slots, width), BF16),
            pltpu.VMEM((2, hosts, back_rows, width), BF16),
            dma((1 + local_count, 2)),
            dma((local_count, 2)),
            dma((2, n - 1)),
            dma((2, n - 1)),
            dma((hosts - 1,)),
            dma((hosts - 1,)),
            dma((2, n - 1)),
            dma((2, n - 1)),
            dma((2, n - 1)),
            dma((2, n - 1)),
            dma((2, local_count, n - 1)),
            dma((2, local_count, n - 1)),
            dma((2, hosts - 1)),
            dma((2, hosts - 1)),
            dma((2 * chips,)),
            dma((2 * chips,)),
            dma((2, chips - 1)),
            dma((2, chips - 1)),
            dma((2,)),
            dma((2,)),
            dma((3,)),
        ],
        compiler_params=pltpu.CompilerParams(
            collective_id=0, has_side_effects=True, vmem_limit_bytes=64 * 2**20 - 2**17
        ),
        name="layer",
    )(
        tokens, cotangent, sendbuf, perm, gate_kept[:, None], kept_float[:, None], pick, unperm,
        residual_in, residual_out, expert_in, expert_out,
    )
    if not reduce_here:
        in_total, out_total = lax.psum((in_total, out_total), "expert")
    return (
        output,
        grad_tokens,
        grad_gate[:, 0],
        grad_expert_in,
        grad_expert_out,
        in_total,
        out_total,
    )


def solution(mesh):
    return jax.shard_map(
        on_device,
        mesh=mesh,
        in_specs=(
            P(("dp", "expert"), None),
            P(("dp", "expert")),
            P(("dp", "expert")),
            P(("dp", "expert")),
            P(("dp", "expert")),
            P(("dp", "expert"), None),
            P("expert", None, "dp"),
            P("expert", "dp", None),
            P(None, "dp"),
            P("dp", None),
        ),
        out_specs=(
            P(("dp", "expert"), None),
            P(("dp", "expert"), None),
            P(("dp", "expert")),
            P("expert", None, "dp"),
            P("expert", "dp", None),
            P(None, "dp"),
            P("dp", None),
        ),
        check_vma=False,
    )
```

time: 265 us -> 217 us (0.82)
  Pallas kernels: 214 us -> 183 us
  matrix products: 24.1 us -> 2.49 us
  local copies, waits for them, and re-layouts: 7.77 us -> 25.1 us
  between operations: 14.1 us -> 0.66 us
    pallas_call x2 -> x1, Pallas kernels: 214 us -> 183 us  [on_device(): pl.pallas_call(functools.partial(layer_kernel, n, hosts, local_count, red...]
    dot_general x2 -> x0, matrix products: 21.6 us -> none  [the longest x1 12.1 us: on_device(): jnp.einsum('njsd,jnsf->jdf', column[:, :local_count], gpre.reshape(local_...]
    unnamed x14 -> x10, local copies, waits for them, and re-layouts: 6.29 us -> 23.7 us
  transfers between devices with their start and end apart: 1 -> 0, of which waited for: 0 -> 0; matrix products, arithmetic and copies ran while one was open for 10% -> 0% of each run, Pallas kernels for 48% -> 0%
where the time goes in v2:
time: 217 us; the launch traced here: 216 us
  Pallas kernels  183 us (84%)
  local copies, waits for them, and re-layouts  25.1 us (12%)
  other arithmetic  4.75 us (2%)
  matrix products  2.49 us (1%)
    pallas_call x1, Pallas kernels, on_device(): pl.pallas_call(functools.partial(layer_kernel, n, hosts, local_count, red...  183 us
    unnamed x10, local copies, waits for them, and re-layouts  23.7 us

profile of v2, /device:TPU:9, one launch (start us, length us, event | category | flops | bytes accessed | tf_op | source)
XLA Modules:
  0.0 216.0 jit_solution(4973727789015763212)
XLA Ops:
  0.6 0.7 add_select_fusion
  1.3 0.7 broadcast_select_fusion
  2.0 0.7 copy.22.kept
  2.8 0.7 fusion.6.pick
  3.5 0.7 copy.21.gate
  4.2 0.1 iota_compare_fusion
  4.3 1.1 multiply_convert_fusion
  5.4 2.5 %convolution_convert_fusion = bf16[384,1536]{1,0:T(8,128)(2,1)} fusion(bf16[128,1536]{1,0:T(8,128)(2,1)S(1)} %multiply_convert_fusion, bf16[128,1536]{1,0:T(8,128)(2,1)} %tok.1, pred[384,128]{1,0:T(32,128)(4,1)S(1)} %get-tuple-element.27, pred[384,128]{1,0:T(32,128)(4,1)S(1)} %get-tuple-element.28), kind=kOutput, calls=%fused_computation | convolution fusion | flops 304250880 | bytes 2064384 | tf_op jit(solution)/shard_map/dot_general | solution.py:18
  7.9 182.9 %layer.1 = (bf16[128,1536]{1,0:T(8,128)(2,1)}, bf16[128,1536]{1,0:T(8,128)(2,1)}, f32[128,1]{1,0:T(8,128)}, bf16[1536,768]{1,0:T(8,128)(2,1)}, bf16[768,1536]{1,...) custom-call(bf16[128,1536]{1,0:T(8,128)(2,1)} %tok.1, bf16[128,1536]{1,0:T(8,128)(2,1)} %cot.1, ...), custom_call_target="tpu_custom_call" | custom-call | tf_op jit(solution)/shard_map/layer/pallas_call | solution.py:420
  190.8 1.5 reduce
  192.3 1.8 copy.33
  194.1 1.8 copy.34
  195.8 8.0 %copy.35 = bf16[2,1536,1536]{2,1,0:T(8,128)(2,1)} copy(bf16[2,1536,1536]{2,1,0:T(8,128)(2,1)} %get-tuple-element.39) | data formatting | bytes 18874368
  203.9 0.0 copy-start.1
  203.9 8.2 %copy.36 = bf16[2,1536,1536]{2,1,0:T(8,128)(2,1)} copy(bf16[2,1536,1536]{2,1,0:T(8,128)(2,1)} %get-tuple-element.40) | data formatting | bytes 18874368
  212.0 0.0 copy-done.1
  212.0 0.0 copy-start
  212.0 1.4 copy.37
  213.4 1.1 copy-done
  214.6 1.4 copy.38
  (2 shorter events, 0.0 us)
Async XLA Ops:
  203.9 8.2 %copy-start.1 = (bf16[1536,768]{1,0:T(8,128)(2,1)S(1)}, bf16[1536,768]{1,0:T(8,128)(2,1)}, u32[]{:S(2)}) copy-start(bf16[1536,768]{1,0:T(8,128)(2,1)} %get-tuple-element.41) | copy-start | bytes 7077892
  212.0 2.5 %copy-start = (bf16[768,1536]{1,0:T(8,128)(2,1)S(1)}, bf16[768,1536]{1,0:T(8,128)(2,1)}, u32[]{:S(2)}) copy-start(bf16[768,1536]{1,0:T(8,128)(2,1)} %get-tuple-element.42) | copy-start | bytes 7077892

commit v3 on v2

--- a/solution.py
+++ b/solution.py
@@ -252,6 +252,8 @@
         push(1, j)
 
     third = []
+    near = lax.div(chip, 2) * 2 + 1 - lax.rem(chip, 2)
+    far = lax.rem(chip + 2, chips)
     if reduce_here:
         saves = []
         for c in second:
@@ -266,8 +268,11 @@
             c = pltpu.make_async_copy(done, o.at[block_of(o, core, chip)], lsem.at[i])
             c.start()
             saves.append(c)
-            for k in range(1, chips):
-                q = lax.rem(chip + k, chips)
+            if chips == 4:
+                partners = (near, far)
+            else:
+                partners = [lax.rem(chip + k, chips) for k in range(1, chips)]
+            for k, q in enumerate(partners, 1):
                 third.append(remote(
                     done, o.at[block_of(o, core, chip)],
                     qsend.at[i, k - 1], qrecv.at[i, k - 1], (dp, q * 2 + core),
@@ -287,6 +292,17 @@
             c = pltpu.make_async_copy(src.at[j], dst.at[j], gsem.at[j, s])
             c.start()
             grads.append(c)
+
+    if reduce_here and chips == 4:
+        for i, (p, r1, r2, s, o) in enumerate(pairs):
+            third[2 * i + 1].wait_recv()
+        third = [third[0], third[2]] + [
+            remote(
+                pair[4].at[block_of(pair[4], core, far)], pair[4].at[block_of(pair[4], core, far)],
+                qsend.at[i, 2], qrecv.at[i, 2], (dp, near * 2 + core),
+            )
+            for i, pair in enumerate(pairs)
+        ]
 
     back_rows = back.shape[2]
     back_all = hosts * back_rows

time: 217 us -> 203 us (0.935)
  Pallas kernels: 183 us -> 170 us
    pallas_call x1, Pallas kernels: 183 us -> 170 us  [on_device(): pl.pallas_call(functools.partial(layer_kernel, n, hosts, local_count, red...]
where the time goes in v3:
time: 203 us
  Pallas kernels  170 us (84%)
  local copies, waits for them, and re-layouts  25.1 us (12%)
  other arithmetic  4.75 us (2%)
  matrix products  2.49 us (1%)
    pallas_call x1, Pallas kernels, on_device(): pl.pallas_call(functools.partial(layer_kernel, n, hosts, local_count, red...  170 us
    unnamed x10, local copies, waits for them, and re-layouts  23.7 us

profile of v3, /device:TPU:9, one launch (start us, length us, event | category | flops | bytes accessed | tf_op | source)
XLA Modules:
  0.0 202.7 jit_solution(5822585212002650571)
XLA Ops:
  0.6 0.7 add_select_fusion
  1.3 0.7 broadcast_select_fusion
  2.0 0.7 copy.22.kept
  2.8 0.7 fusion.6.pick
  3.5 0.7 copy.21.gate
  4.2 0.1 iota_compare_fusion
  4.3 1.1 multiply_convert_fusion
  5.4 2.5 %convolution_convert_fusion = bf16[384,1536]{1,0:T(8,128)(2,1)} fusion(bf16[128,1536]{1,0:T(8,128)(2,1)S(1)} %multiply_convert_fusion, bf16[128,1536]{1,0:T(8,128)(2,1)} %tok.1, pred[384,128]{1,0:T(32,128)(4,1)S(1)} %get-tuple-element.27, pred[384,128]{1,0:T(32,128)(4,1)S(1)} %get-tuple-element.28), kind=kOutput, calls=%fused_computation | convolution fusion | flops 304250880 | bytes 2064384 | tf_op jit(solution)/shard_map/dot_general | solution.py:18
  7.9 169.7 %layer.1 = (bf16[128,1536]{1,0:T(8,128)(2,1)}, bf16[128,1536]{1,0:T(8,128)(2,1)}, f32[128,1]{1,0:T(8,128)}, bf16[1536,768]{1,0:T(8,128)(2,1)}, bf16[768,1536]{1,...) custom-call(bf16[128,1536]{1,0:T(8,128)(2,1)} %tok.1, bf16[128,1536]{1,0:T(8,128)(2,1)} %cot.1, ...), custom_call_target="tpu_custom_call" | custom-call | tf_op jit(solution)/shard_map/layer/pallas_call | solution.py:436
  177.6 1.5 reduce
  179.1 1.8 copy.33
  180.8 1.8 copy.34
  182.6 8.0 %copy.35 = bf16[2,1536,1536]{2,1,0:T(8,128)(2,1)} copy(bf16[2,1536,1536]{2,1,0:T(8,128)(2,1)} %get-tuple-element.39) | data formatting | bytes 18874368
  190.6 0.0 copy-start.1
  190.6 8.2 %copy.36 = bf16[2,1536,1536]{2,1,0:T(8,128)(2,1)} copy(bf16[2,1536,1536]{2,1,0:T(8,128)(2,1)} %get-tuple-element.40) | data formatting | bytes 18874368
  198.8 0.0 copy-done.1
  198.8 0.0 copy-start
  198.8 1.4 copy.37
  200.2 1.1 copy-done
  201.3 1.4 copy.38
  (2 shorter events, 0.0 us)
Async XLA Ops:
  190.6 8.2 %copy-start.1 = (bf16[1536,768]{1,0:T(8,128)(2,1)S(1)}, bf16[1536,768]{1,0:T(8,128)(2,1)}, u32[]{:S(2)}) copy-start(bf16[1536,768]{1,0:T(8,128)(2,1)} %get-tuple-element.41) | copy-start | bytes 7077892
  198.8 2.5 %copy-start = (bf16[768,1536]{1,0:T(8,128)(2,1)S(1)}, bf16[768,1536]{1,0:T(8,128)(2,1)}, u32[]{:S(2)}) copy-start(bf16[768,1536]{1,0:T(8,128)(2,1)} %get-tuple-element.42) | copy-start | bytes 7077892
